TPU v7x, 128 devices: a whole 4x4x4 slice. The times are simulated.
128 devices in a mesh: rep: 8 (over y, core), tp: 16 (over x, z).
Axes of the slice: x: 4, y: 4, z: 4, core: 2. Of those that a mesh axis runs over, the one named last changes fastest.
Arguments:
- learner_rows: bfloat16 [18432, 8192], P(('rep', 'tp'))
- learner_slot: int32 [18432], replicated, may hold values from 0 to 18431, as said below
- query_order: int32 [128], replicated, may hold values from 0 to 127, each once
- kv_order: int32 [16], replicated, may hold values from 0 to 7, as said below
- tokens: bfloat16 [8192, 8192], P(('rep', 'tp')), may hold values from -6 to 6
- positions: int32 [8192], P('rep'), may hold values from 0 to 5118, as said below
Outputs:
- refit_weight: bfloat16 [20480, 8192], P('tp')
- qkv_rope: bfloat16 [8192, 20480], P('rep', 'tp')
Inputs may be any that keep to these rules, and one draw needn't show every extreme that they name: learner_slot is a permutation of the 18432 slots; the learner device with index d (rep major) holds slots d * 144 to (d + 1) * 144 - 1, and within that block the slots h * 1 to (h + 1) - 1 hold rows of joined head block h, that is of rows h * 128 to (h + 1) * 128 - 1. `kv_order`: each key-value head appears exactly 16/8 times. `positions`: within each replica's block of 1024 tokens a position is one more than the one before, or 0 where a document begins; the first token of a block has a position below 4096; one replica's block begins at 4095 and has no document start, and the next replica's block has a document start at token 512.
All inputs are finite; a program needn't handle non-finite values.
Results may differ from a plain program's by a relative error of at most 0.0049.
Values may be sent and summed in bfloat16 or wider, within the bound.
A program may use at most 256 MiB of HBM per device.

v0:
```python
import math

import jax
import jax.numpy as jnp
from jax import lax
from jax.sharding import PartitionSpec as P

HD = 128
QH = 128
KVH = 8


epsilon = 1e-06
rope_base = 500000.0


def rotate(values, place_ids, head_total, group_size):
    row_total = values.shape[0]
    half_dim = HD // 2
    frequency = jnp.exp(jnp.arange(half_dim, dtype=jnp.float32) * (-2.0 * math.log(rope_base) / HD))
    angles = place_ids.astype(jnp.float32)[:, None] * frequency[None, :]
    cosines = jnp.cos(angles)[:, None, :]
    sines = jnp.sin(angles)[:, None, :]
    shaped = values.reshape(row_total, head_total, HD)
    lower_half = shaped[:, :, :half_dim]
    upper_half = shaped[:, :, half_dim:]
    turned = jnp.concatenate(
        [lower_half * cosines - upper_half * sines, upper_half * cosines + lower_half * sines],
        axis=2,
    )
    keep_value = (jnp.arange(head_total) % group_size == group_size - 1)[None, :, None]
    return jnp.where(keep_value, shaped, turned).reshape(row_total, head_total * HD)


def per_device(learner_rows, learner_slot, query_order, kv_order, tokens, positions):
    tp_count = lax.axis_size("tp")
    rep_count = lax.axis_size("rep")
    devices = tp_count * rep_count
    row_width = learner_rows.shape[1]
    per_head = HD // devices
    head_total = learner_rows.shape[0] // per_head
    largest = jnp.max(jnp.abs(learner_rows), axis=1).astype(jnp.float32)
    row_scale = (largest + epsilon).astype(jnp.bfloat16)
    quantized = (learner_rows.astype(jnp.float32) / row_scale.astype(jnp.float32)[:, None]).astype(
        jnp.bfloat16
    )
    query_per = query_order.shape[0] // tp_count
    head_table = jnp.concatenate(
        [
            query_order.reshape(tp_count, query_per),
            QH + kv_order[:, None],
            QH + KVH + kv_order[:, None],
        ],
        axis=1,
    )
    group_size = head_table.shape[1]
    selector = (
        head_table.reshape(-1)[:, None] == jnp.arange(head_total, dtype=jnp.int32)[None, :]
    ).astype(jnp.bfloat16)
    send_rows = jnp.dot(selector, quantized, preferred_element_type=jnp.float32)
    send_rows = send_rows.astype(jnp.bfloat16).reshape(tp_count, group_size, per_head, row_width)
    send_scale = jnp.take(row_scale.reshape(head_total, per_head), head_table, axis=0)
    part_rows, part_scale = (
        lax.all_to_all(send_rows, "tp", split_axis=0, concat_axis=2, tiled=True),
        lax.all_to_all(send_scale, "tp", split_axis=0, concat_axis=2, tiled=True),
    )
    got_rows, got_scale = (
        lax.all_gather(part_rows, "rep", axis=2, tiled=True),
        lax.all_gather(part_scale, "rep", axis=2, tiled=True),
    )
    my_index = lax.axis_index("tp")
    my_heads = lax.dynamic_index_in_dim(head_table, my_index, 0, keepdims=False)
    joined_ids = my_heads[:, None] * HD + jnp.arange(HD, dtype=jnp.int32)[None, :]
    slot_ids = jnp.take(learner_slot, joined_ids.reshape(-1)).reshape(group_size, HD)
    rows_dev = head_total * per_head
    source_dev = slot_ids // rows_dev
    within_head = slot_ids % per_head
    flat_index = source_dev * per_head + within_head
    picker = (flat_index[:, :, None] == jnp.arange(HD, dtype=jnp.int32)[None, None, :]).astype(
        jnp.bfloat16
    )
    placed = jnp.einsum("gjk,gkc->gjc", picker, got_rows[0], preferred_element_type=jnp.float32)
    refit_weight = placed.astype(jnp.bfloat16).reshape(group_size * HD, row_width)
    column_scale = (
        jnp.take_along_axis(got_scale[0], flat_index, axis=1).reshape(-1).astype(jnp.float32)
    )
    product = lax.dot_general(
        lax.all_gather(tokens, "tp", axis=0, tiled=True),
        refit_weight,
        (((1,), (1,)), ((), ())),
        preferred_element_type=jnp.float32,
    )
    qkv_rope = rotate(product * column_scale[None, :], positions, group_size, group_size).astype(
        jnp.bfloat16
    )
    return (refit_weight, qkv_rope)


def solution(mesh):
    in_specs = (P(("rep", "tp"), None), P(), P(), P(), P(("rep", "tp"), None), P("rep"))
    out_specs = (P("tp", None), P("rep", "tp"))
    return jax.shard_map(
        per_device, mesh=mesh, in_specs=in_specs, out_specs=out_specs, check_vma=False
    )
```

profile of v0, /device:TPU:1, one launch (start us, length us, event | category | flops | bytes accessed | tf_op | source)
XLA Modules:
  0.0 333.7 jit_solution(2361657101497172343)
XLA Ops:
  7.2 0.0 copy-start
  7.2 0.0 all-gather.7.cloned.1.call-start
  7.2 0.7 add_bitcast_fusion.2
  7.9 0.1 copy.28
  8.0 0.1 copy.29
  8.1 0.7 reshape.536
  8.8 2.2 abs_reduce_fusion
  11.0 0.1 pad_add_fusion
  11.0 0.1 eq.42
  11.1 2.6 convolution_convert_fusion
  13.7 2.8 reshape.537
  16.5 57.6 %all_to_all.36 = bf16[16,10,1,8192]{3,1,2,0:T(8,128)(2,1)S(1)} all-to-all(bf16[16,10,1,8192]{3,1,2,0:T(8,128)(2,1)} %bitcast.100), channel_id=1, replica_groups=mesh['rep'=8,'tp'=16] {'tp'}, dimensions={0} | all-to-all | bytes 5242880 | tf_op jit(solution)/shard_map/all_to_all | solution.py:64
  74.2 2.9 copy.41
  77.1 0.0 all-gather.7.cloned.1.call-update
  77.1 0.0 copy-start.2
  77.1 0.0 all-gather.5.cloned.1.call-start
  77.2 0.7 all-gather.5.cloned.1.call-update
  77.9 0.0 copy-done.3
  77.9 0.1 concatenate.48
  78.0 0.1 copy.32
  78.1 0.1 copy.33
  78.1 0.1 compare_select_fusion.3
  78.2 0.1 reshape.552
  78.3 1.6 gather_fusion.1
  79.9 0.1 reshape.549
  80.0 0.1 and_select_fusion
  80.1 0.6 copy.34
  80.7 4.5 %all-to-all-start.1 = ((bf16[16,10,1]{1,2,0:T(2,128)(2,1)}), bf16[16,10,1]{1,2,0:T(2,128)(2,1)S(1)}, u32[]{:S(2)}, u32[]{:S(2)}) async-start(bf16[16,10,1]{1,2,0:T(2,128)(2,1)} %copy.34), calls=%async_computation.1 | async-start | bytes 16384 | tf_op jit(solution)/shard_map/all_to_all | solution.py:65
  85.3 0.1 fusion.17
  85.4 7.1 %gather_fusion = s32[1280]{0:T(1024)S(1)} fusion(s32[18432]{0:T(1024)S(1)} %copy-done, s32[2048]{0:T(1024)S(1)} %pad_clamp_fusion), kind=kCustom, calls=%fused_computation | custom fusion | bytes 15360 | tf_op jit(solution)/shard_map/jit(_take)/gather | solution.py:74
  92.5 0.1 fusion.12
  92.6 0.1 add_select_fusion.2
  92.7 1.0 multiply_cosine_fusion
  93.7 0.1 broadcast_bitcast_fusion
  93.8 0.0 all-to-all-done.1
  93.8 15.5 %all-gather.1 = bf16[1,10,128,1]{1,2,3,0:T(8,128)(2,1)S(1)} all-gather(bf16[1,10,16,1]{1,2,3,0:T(8,128)(2,1)S(1)} %bitcast.102), channel_id=3, replica_groups=mesh['rep'=8,'tp'=16] {'rep'}, dimensions={2}, use_global_device_ids=true | all-gather | bytes 2880 | tf_op jit(solution)/shard_map/all_gather | solution.py:69
  109.3 10.5 %gather_fusion.2 = bf16[1280]{0:T(1024)(128)(2,1)S(1)} fusion(bf16[10,128]{0,1:T(8,128)(2,1)S(1)} %bitcast.96, s32[1280]{0:T(1024)S(1)} %fusion.12), kind=kCustom, calls=%fused_computation.2 | custom fusion | bytes 15360 | tf_op jit(solution)/shard_map/jit(take_along_axis)/gather | solution.py:85
  119.7 0.1 fusion.28
  119.8 61.1 %all-gather.7.cloned.1.call-done = bf16[1,10,128,1,8192]{4,2,1,3,0:T(8,128)(2,1)} async-done(((bf16[1,10,16,1,8192]{4,2,1,3,0:T(8,128)(2,1)}), bf16[1,10,128,1,8192]{4,2,1,3,0:T(8,128)(2,1)}) %all-gather.7.cloned.1.call-update) | async-done | bytes 20971536 | tf_op jit(solution)/shard_map/all_gather | solution.py:68
  180.9 19.3 %fusion.2 = bf16[10,128,8192]{2,1,0:T(8,128)(2,1)} fusion(bf16[1,10,128,1,8192]{4,2,1,3,0:T(8,128)(2,1)} %all-gather.7.cloned.1.call-done, s32[10,128]{1,0:T(8,128)S(1)} %add_select_fusion.2), kind=kOutput, calls=%fused_computation.5 | convolution fusion | flops 2695004160 | bytes 41948160 | tf_op jit(solution)/shard_map/gjk,gkc->gjc/dot_general | solution.py:82
  200.2 94.7 %all-gather.5.cloned.1.call-done = bf16[1024,8192]{1,0:T(8,128)(2,1)} async-done(((bf16[64,8192]{1,0:T(8,128)(2,1)}), bf16[1024,8192]{1,0:T(8,128)(2,1)}) %all-gather.5.cloned.1.call-update) | async-done | bytes 16777232 | tf_op jit(solution)/shard_map/all_gather | solution.py:88
  294.9 27.3 %convolution_multiply_fusion = f32[1280,1024]{1,0:T(8,128)S(1)} fusion(bf16[1280,8192]{1,0:T(8,128)(2,1)} %bitcast.97, bf16[1024,8192]{1,0:T(8,128)(2,1)} %all-gather.5.cloned.1.call-done, f32[1280]{0:T(1024)S(1)} %fusion.28), kind=kOutput, calls=%fused_computation.7 | convolution fusion | flops 21476147200 | bytes 42996736 | tf_op jit(solution)/shard_map/dot_general | solution.py:87
  322.2 0.9 multiply_subtract_fusion
  323.2 0.2 pad_maximum_fusion
  323.4 0.0 copy-start.1
  323.4 0.7 fusion.5
  324.2 2.7 copy.35
  326.9 0.0 copy-done.1
  (12 shorter events, 0.1 us)
Async XLA Ops:
  7.2 78.2 %copy-start = (s32[18432]{0:T(1024)S(1)}, s32[18432]{0:T(1024)}, u32[]{:S(2)}) copy-start(s32[18432]{0:T(1024)} %param.7) | copy-start | bytes 221188
  7.2 173.7 %all-gather.7.cloned.1.call-start = ((), (), s32[]{:S(2)}) async-start(), calls=%async_computation.3 | async-start | bytes 23592960 | tf_op jit(solution)/shard_map/all_gather | solution.py:68
  77.1 0.8 copy-start.3
  77.1 8.1 %copy-start.2 = (s32[1024]{0:T(1024)S(1)}, s32[1024]{0:T(1024)}, u32[]{:S(2)}) copy-start(s32[1024]{0:T(1024)} %param.11) | copy-start | bytes 12292
  77.1 217.8 %all-gather.5.cloned.1.call-start = ((), (), s32[]{:S(2)}) async-start(), calls=%async_computation.2 | async-start | bytes 17825792 | tf_op jit(solution)/shard_map/all_gather | solution.py:88
  80.7 13.1 %all-to-all-start.1 = ((bf16[16,10,1]{1,2,0:T(2,128)(2,1)}), bf16[16,10,1]{1,2,0:T(2,128)(2,1)S(1)}, u32[]{:S(2)}, u32[]{:S(2)}) async-start(bf16[16,10,1]{1,2,0:T(2,128)(2,1)} %copy.34), calls=%async_computation.1 | async-start | bytes 16384 | tf_op jit(solution)/shard_map/all_to_all | solution.py:65
  323.4 3.4 %copy-start.1 = (s32[18432]{0:T(1024)S(1)}, s32[18432]{0:T(1024)}, u32[]{:S(2)}) copy-start(s32[18432]{0:T(1024)} %param.7) | copy-start | bytes 221188
Sparse Core Ops, SparseCore 0:
  77.2 103.6 all-gather.6
  183.0 111.8 all-gather.4
where the time goes:
time: 334 us
  waiting for transfers between devices  156 us (47%)
  blocking collectives  73.1 us (22%)
  matrix products  49.3 us (15%)
  local copies, waits for them, and re-layouts  29.7 us (9%)
  between operations  14.2 us (4%)
  other arithmetic  6.36 us (2%)
  starting transfers between devices  4.61 us (1%)
    all_gather x1, waiting for transfers between devices, per_device(): lax.all_gather(tokens, 'tp', axis=0, tiled=True)  94.7 us
    all_gather x1, waiting for transfers between devices, per_device(): lax.all_gather(part_rows, 'rep', axis=2, tiled=True)  61.1 us
    all_to_all x1, blocking collectives, per_device(): lax.all_to_all(send_rows, 'tp', split_axis=0, concat_axis=2, tiled=True)  57.6 us
    dot_general x1, matrix products, per_device(): lax.dot_general(lax.all_gather(tokens, 'tp', axis=0, tiled=True), refit_w...  27.3 us
    dot_general x1, matrix products, per_device(): jnp.einsum('gjk,gkc->gjc', picker, got_rows[0], preferred_element_type=jn...  19.3 us
    all_gather x1, blocking collectives, per_device(): lax.all_gather(part_scale, 'rep', axis=2, tiled=True)  15.5 us
    gather x1, local copies, waits for them, and re-layouts, per_device(): jnp.take_along_axis(got_scale[0], flat_index, axis=1).reshape(-1)  10.5 us
    gather x1, local copies, waits for them, and re-layouts, per_device(): jnp.take(learner_slot, joined_ids.reshape(-1)).reshape(group_size, HD)  7.08 us
  transfers between devices with their start and end apart: 3, of which 2 were waited for; matrix products, arithmetic and copies ran while one was open for 12% of the time, Pallas kernels for 0%

commit v1 on v0

v1 whole, which is shorter than its diff:
```python
import functools
import math

import jax
import jax.numpy as jnp
from jax import lax
from jax.experimental import pallas as pl
from jax.experimental.pallas import tpu as pltpu
from jax.sharding import PartitionSpec as P

HD = 128
QH = 128
KVH = 8
HEADS = 144
GROUP = 10
DW = 8192
SPAN = 1024
ROWS = 64
PAIRS = 5
SUB = 1024
QS = DW // SUB
HALF = DW // 2
WIDE = PAIRS * SUB + 128
SLOTS = 2048

epsilon = 1e-06
rope_base = 500000.0
MESH = pl.DeviceIdType.MESH


def columns_of(pair):
    if pair == 0:
        return pl.ds(0, SUB + 128)
    return pl.ds(128 + pair * SUB, SUB)


def data_of(pair):
    return pl.ds(128 + pair * SUB, SUB)


def exchange(
    tokens,
    learner,
    slots,
    query_row,
    kv_row,
    query_s,
    kv_s,
    all_tokens,
    placed,
    scales,
    rows,
    stacked,
    sending,
    slab,
    stage,
    turned,
    t_send,
    t_recv,
    w_send,
    w_recv,
    a_send,
    a_recv,
    c_recv,
    l_sem,
    s_sem,
):
    rep = lax.axis_index("rep")
    tp = lax.axis_index("tp")
    y, core = rep // 2, rep % 2
    x, z = tp // 4, tp % 4

    def place_of(dx, dz):
        return lax.rem(x + dx + 4, 4) * 4 + lax.rem(z + dz + 4, 4)

    def rep_of(dy):
        return lax.rem(y + dy + 4, 4) * 2 + core

    twin = y * 2 + 1 - core

    load_rows = pltpu.make_async_copy(learner, rows, l_sem.at[0])
    load_rows.start()
    own_copy = pltpu.make_async_copy(tokens, all_tokens.at[tp], l_sem.at[1])
    own_copy.start()

    barrier = pltpu.get_barrier_semaphore()
    offsets = [(dx, dz) for dx in (1, 3, 0, 2) for dz in (1, 3, 0, 2) if (dx, dz) != (0, 0)]
    for dx, dz in offsets:
        pl.semaphore_signal(barrier, inc=1, device_id=(rep, place_of(dx, dz)), device_id_type=MESH)
    for other in (rep_of(1), rep_of(3), twin):
        pl.semaphore_signal(barrier, inc=1, device_id=(other, tp), device_id_type=MESH)
    pl.semaphore_wait(barrier, len(offsets) + 3)

    def along(half, phase, step):
        return place_of(step, 0) if (half == 0) == (phase == 0) else place_of(0, step)

    def block_at(half, first, second):
        return place_of(first, second) if half == 0 else place_of(second, first)

    def piece(ref, half, low, count):
        return ref.at[pl.ds(low, count), pl.ds(half * HALF, HALF)]

    started = []

    def token_copy(half, number, block, low, count, phase, step, own=False):
        k = half * 20 + number
        source = piece(tokens, half, low, count) if own else piece(all_tokens.at[block], half, low, count)
        copy = pltpu.make_async_remote_copy(
            src_ref=source,
            dst_ref=piece(all_tokens.at[block], half, low, count),
            send_sem=t_send.at[k],
            recv_sem=t_recv.at[k],
            device_id=(rep, along(half, phase, step)),
            device_id_type=MESH,
        )
        copy.start()
        started.append(copy)

    def token_wait(half, number, block, low, count):
        k = half * 20 + number
        here = piece(all_tokens.at[block], half, low, count)
        pltpu.make_async_copy(here, here, t_recv.at[k]).wait()

    def first_sends():
        for half in (0, 1):
            token_copy(half, 0, tp, 0, ROWS, 0, 1, own=True)
            token_copy(half, 1, tp, 0, ROWS, 0, -1, own=True)

    order = (0, -1, 1, 2)

    def second_sends(half, k):
        block = block_at(half, order[k], 0)
        token_copy(half, 4 + 4 * k, block, 0, ROWS, 1, 1, own=k == 0)
        token_copy(half, 5 + 4 * k, block, 0, ROWS, 1, -1, own=k == 0)

    def token_step(number):
        for half in (0, 1):
            if number == 0:
                second_sends(half, 0)
            elif number == 1:
                block = block_at(half, -1, 0)
                token_wait(half, 0, block, 0, ROWS)
                token_copy(half, 2, block, 0, ROWS // 2, 0, 1)
                second_sends(half, 1)
            elif number == 2:
                block = block_at(half, 1, 0)
                token_wait(half, 1, block, 0, ROWS)
                token_copy(half, 3, block, ROWS // 2, ROWS // 2, 0, -1)
                second_sends(half, 2)
            elif number == 3:
                block = block_at(half, 2, 0)
                token_wait(half, 2, block, 0, ROWS // 2)
                token_wait(half, 3, block, ROWS // 2, ROWS // 2)
                second_sends(half, 3)
            elif number < 8:
                k = number - 4
                block = block_at(half, order[k], -1)
                token_wait(half, 4 + 4 * k, block, 0, ROWS)
                token_copy(half, 6 + 4 * k, block, 0, ROWS // 2, 1, 1)
                block = block_at(half, order[k], 1)
                token_wait(half, 5 + 4 * k, block, 0, ROWS)
                token_copy(half, 7 + 4 * k, block, ROWS // 2, ROWS // 2, 1, -1)
            else:
                k = number - 8
                block = block_at(half, order[k], 2)
                token_wait(half, 6 + 4 * k, block, 0, ROWS // 2)
                token_wait(half, 7 + 4 * k, block, ROWS // 2, ROWS // 2)

    def block_rows(core_, y_, low=0, count=256):
        return pl.ds(pl.multiple_of((core_ * 4 + y_) * 256, 256) + low, count)

    mine = block_rows(core, y)

    def weight_copy(pair, number, rows_, recv, device):
        k = pair * 8 + number
        here = slab.at[rows_, columns_of(pair)]
        copy = pltpu.make_async_remote_copy(
            src_ref=here, dst_ref=here, send_sem=w_send.at[k], recv_sem=recv, device_id=device, device_id_type=MESH
        )
        copy.start()
        started.append(copy)

    def weight_wait(pair, rows_, sem):
        here = slab.at[rows_, columns_of(pair)]
        pltpu.make_async_copy(here, here, sem).wait()

    def scatter(pair):
        for dx, dz in offsets:
            to = place_of(dx, dz)
            pltpu.make_async_remote_copy(
                src_ref=sending.at[pl.ds(pl.multiple_of(to * 16, 16), 16), columns_of(pair)],
                dst_ref=slab.at[
                    pl.ds(pl.multiple_of((core * 4 + y) * 256 + tp * 16, 16), 16), columns_of(pair)
                ],
                send_sem=a_send.at[pair],
                recv_sem=a_recv.at[pair],
                device_id=(rep, to),
                device_id_type=MESH,
            ).start()
        pltpu.make_async_copy(
            sending.at[pl.ds(pl.multiple_of(tp * 16, 16), 16), columns_of(pair)],
            slab.at[pl.ds(pl.multiple_of((core * 4 + y) * 256 + tp * 16, 16), 16), columns_of(pair)],
            s_sem.at[pair],
        ).start()

    ym, yp, y2 = lax.rem(y + 3, 4), lax.rem(y + 1, 4), lax.rem(y + 2, 4)
    up, down, across = (rep_of(1), tp), (rep_of(-1), tp), (twin, tp)

    def gathered(pair):
        fifteen = slab.at[block_rows(core, y, 0, 240), columns_of(pair)]
        pltpu.make_async_copy(fifteen, fifteen, a_recv.at[pair]).wait()
        one = slab.at[block_rows(core, y, 0, 16), columns_of(pair)]
        pltpu.make_async_copy(one, one, s_sem.at[pair]).wait()
        weight_copy(pair, 0, mine, w_recv.at[pair * 4], up)
        weight_copy(pair, 1, mine, w_recv.at[pair * 4 + 1], down)
        weight_copy(pair, 4, mine, c_recv.at[pair], across)

    def relayed(pair):
        weight_wait(pair, block_rows(core, ym), w_recv.at[pair * 4])
        weight_copy(pair, 2, block_rows(core, ym, 0, 128), w_recv.at[pair * 4 + 2], up)
        weight_copy(pair, 5, block_rows(core, ym), c_recv.at[pair], across)
        weight_wait(pair, block_rows(core, yp), w_recv.at[pair * 4 + 1])
        weight_copy(pair, 3, block_rows(core, yp, 128, 128), w_recv.at[pair * 4 + 3], down)
        weight_copy(pair, 6, block_rows(core, yp), c_recv.at[pair], across)

    def opposite(pair):
        weight_wait(pair, block_rows(core, y2, 0, 128), w_recv.at[pair * 4 + 2])
        weight_wait(pair, block_rows(core, y2, 128, 128), w_recv.at[pair * 4 + 3])
        weight_copy(pair, 7, block_rows(core, y2), c_recv.at[pair], across)

    def crossed(pair):
        weight_wait(pair, pl.ds(pl.multiple_of((1 - core) * 1024, 1024), 1024), c_recv.at[pair])

    def place(pair):
        buffer = pair % 2
        if pair >= 2:
            stored(pair - 2).wait()

        def columns(q, carry):
            lane = lax.broadcasted_iota(jnp.int32, (HD, SLOTS), 1)
            parts = []
            for i in (0, 1):
                want = turned[:, pl.ds(2 * pair + i, 1)] + (2 * q + i)
                parts.append(jnp.where(lane == want, 1.0, 0.0).astype(jnp.bfloat16))
            picker = jnp.concatenate(parts, axis=0)
            stage[buffer, :, pl.ds(pl.multiple_of(q * SUB, SUB), SUB)] = jnp.dot(
                picker, slab[:, data_of(pair)], preferred_element_type=jnp.float32
            ).astype(jnp.bfloat16)

            @pl.when(q == 0)
            def _():
                scales[pl.ds(pair * 256, 256), :] = jnp.dot(
                    picker, slab[:, pl.ds(0, 128)], preferred_element_type=jnp.float32
                )

            return carry

        lax.fori_loop(0, QS, columns, 0)
        stored(pair).start()

    def stored(pair):
        return pltpu.make_async_copy(
            stage.at[pair % 2], placed.at[pl.ds(pair * 256, 256)], l_sem.at[2 + pair % 2]
        )

    first_sends()
    load_rows.wait()

    largest = jnp.zeros((HEADS, 1), jnp.float32)
    for q in range(QS):
        part = jnp.abs(rows[:, pl.ds(q * SUB, SUB)].astype(jnp.float32))
        largest = jnp.maximum(largest, jnp.max(part, axis=1, keepdims=True))
    row_scale = (largest + epsilon).astype(jnp.bfloat16)
    scale = row_scale.astype(jnp.float32)
    for q in range(QS):
        stacked[pl.ds(q * HEADS, HEADS), :] = (
            rows[:, pl.ds(q * SUB, SUB)].astype(jnp.float32) / scale
        ).astype(jnp.bfloat16)
    wide_scale = jnp.broadcast_to(scale, (HEADS, 128)).astype(jnp.bfloat16)

    def head_column(pair):
        row = lax.broadcasted_iota(jnp.int32, (256, 128), 0)
        lane = lax.broadcasted_iota(jnp.int32, (256, 128), 1)
        u, i = row // 16, row % 2
        if pair < 4:
            chosen = jnp.where(lane == u * 8 + 2 * pair + i, query_row[0:1, :], 0)
            return jnp.sum(chosen.astype(jnp.float32), axis=1, keepdims=True).astype(jnp.int32)
        chosen = jnp.where(lane == u, kv_row[0:1, :] + QH + KVH * i, 0)
        return jnp.sum(chosen.astype(jnp.float32), axis=1, keepdims=True).astype(jnp.int32)

    heads = [head_column(pair) for pair in range(PAIRS)]
    tile = jnp.zeros((256, 128), jnp.float32)
    lane = lax.broadcasted_iota(jnp.int32, (256, HEADS), 1)
    lane128 = lax.broadcasted_iota(jnp.int32, (256, 128), 1)
    for pair in range(PAIRS):
        pick = jnp.where(lane == heads[pair], 1.0, 0.0).astype(jnp.bfloat16)
        got = jnp.dot(pick, wide_scale, preferred_element_type=jnp.float32)
        tile = jnp.where(lane128 == pair, got, tile)
    sending[:, pl.ds(0, 128)] = tile.astype(jnp.bfloat16)

    def prepare(pair):
        piece_of = (lax.broadcasted_iota(jnp.int32, (256, 1), 0) // 2) % QS
        want = heads[pair] + piece_of * HEADS
        lanes = lax.broadcasted_iota(jnp.int32, (256, QS * HEADS), 1)
        pick = jnp.where(lanes == want, 1.0, 0.0).astype(jnp.bfloat16)
        sending[:, data_of(pair)] = jnp.dot(
            pick, stacked[...], preferred_element_type=jnp.float32
        ).astype(jnp.bfloat16)

    for pair in range(PAIRS):
        prepare(pair)
        scatter(pair)
        if pair == 1:
            token_step(0)

    turned[...] = jnp.zeros_like(turned)
    for i in range(GROUP):
        if i < 8:
            head = query_s[tp * 8 + i]
        else:
            head = kv_s[tp] + QH + KVH * (i - 8)
        slot = slots[pl.ds(head, 1), :]
        source = ((slot.astype(jnp.float32) + 0.5) * (1.0 / HEADS)).astype(jnp.int32)
        at = ((source // 16) % 2 * 4 + source // 32) * 256 + (source % 16) * 16
        turned[i : i + 1, :] = at
    turned[...] = jnp.transpose(turned[...].astype(jnp.float32)).astype(jnp.int32)

    gathered(0)
    token_step(1)
    gathered(1)
    token_step(2)
    relayed(0)
    gathered(2)
    token_step(3)
    opposite(0)
    relayed(1)
    gathered(3)
    crossed(0)
    place(0)
    token_step(4)
    opposite(1)
    relayed(2)
    gathered(4)
    crossed(1)
    place(1)
    token_step(5)
    opposite(2)
    relayed(3)
    crossed(2)
    place(2)
    token_step(6)
    token_step(8)
    opposite(3)
    relayed(4)
    crossed(3)
    place(3)
    token_step(7)
    token_step(9)
    opposite(4)
    crossed(4)
    place(4)
    token_step(10)
    token_step(11)

    own_copy.wait()
    stored(3).wait()
    stored(4).wait()
    for copy in started:
        copy.wait_send()
    for pair in range(PAIRS):
        fifteen = sending.at[pl.ds(0, 240), columns_of(pair)]
        pltpu.make_async_copy(fifteen, fifteen, a_send.at[pair]).wait()


def project(tokens, weight, scales, cosines, sines, refit, out, held, t_sem, r_sem):
    pair = pl.program_id(0)

    def load(k):
        return pltpu.make_async_copy(
            tokens.at[pl.ds(k * 256, 256)], held.at[pl.ds(k * 256, 256)], t_sem.at[k]
        )

    @pl.when(pair == 0)
    def _():
        for k in range(4):
            load(k).start()

    keep = pltpu.make_async_copy(weight, refit.at[pl.ds(pl.multiple_of(pair * 256, 256), 256)], r_sem)
    keep.start()

    lane = lax.broadcasted_iota(jnp.int32, (8, 128), 1)
    chosen = jnp.where(lane == pair, 1.0, 0.0).astype(jnp.bfloat16)
    column_scale = lax.dot_general(
        chosen,
        scales[...].astype(jnp.bfloat16),
        (((1,), (1,)), ((), ())),
        preferred_element_type=jnp.float32,
    )[0:1, :]

    for k in range(4):

        @pl.when(pair == 0)
        def _():
            load(k).wait()

        rows = pl.ds(k * 256, 256)
        product = lax.dot_general(
            held[rows, :], weight[...], (((1,), (1,)), ((), ())), preferred_element_type=jnp.float32
        )
        product = product * column_scale
        for i in (0, 1):
            part = product[:, i * HD : (i + 1) * HD]
            turn = part * cosines[rows, :] + pltpu.roll(part, HD // 2, 1) * sines[rows, :]
            if i == 1:
                turn = jnp.where(pair == PAIRS - 1, part, turn)
            out[rows, pl.ds(i * HD, HD)] = turn.astype(jnp.bfloat16)
    keep.wait()


def per_device(learner_rows, learner_slot, query_order, kv_order, tokens, positions):
    any_space = pl.BlockSpec(memory_space=pl.ANY)
    vmem = pl.BlockSpec(memory_space=pltpu.VMEM)
    smem = pl.BlockSpec(memory_space=pltpu.SMEM)
    dma = pltpu.SemaphoreType.DMA
    all_tokens, placed, scales = pl.pallas_call(
        exchange,
        out_shape=(
            jax.ShapeDtypeStruct((16, ROWS, DW), jnp.bfloat16),
            jax.ShapeDtypeStruct((GROUP * HD, DW), jnp.bfloat16),
            jax.ShapeDtypeStruct((GROUP * HD, 128), jnp.float32),
        ),
        in_specs=[any_space, any_space, vmem, vmem, vmem, smem, smem],
        out_specs=(any_space, any_space, vmem),
        scratch_shapes=[
            pltpu.VMEM((HEADS, DW), jnp.bfloat16),
            pltpu.VMEM((QS * HEADS, SUB), jnp.bfloat16),
            pltpu.VMEM((256, WIDE), jnp.bfloat16),
            pltpu.VMEM((SLOTS, WIDE), jnp.bfloat16),
            pltpu.VMEM((2, 256, DW), jnp.bfloat16),
            pltpu.VMEM((HD, HD), jnp.int32),
            dma((40,)),
            dma((40,)),
            dma((40,)),
            dma((20,)),
            dma((PAIRS,)),
            dma((PAIRS,)),
            dma((PAIRS,)),
            dma((4,)),
            dma((PAIRS,)),
        ],
        compiler_params=pltpu.CompilerParams(
            collective_id=0, has_side_effects=True, vmem_limit_bytes=56 * 2**20
        ),
    )(
        tokens,
        learner_rows,
        learner_slot.reshape(HEADS, HD),
        query_order.reshape(1, QH),
        jnp.pad(kv_order, (0, 128 - kv_order.shape[0])).reshape(1, 128),
        query_order,
        kv_order,
    )

    half = HD // 2
    frequency = jnp.exp(jnp.arange(half, dtype=jnp.float32) * (-2.0 * math.log(rope_base) / HD))
    angles = positions.astype(jnp.float32)[:, None] * frequency[None, :]
    cosines, sines = jnp.cos(angles), jnp.sin(angles)
    cosines = jnp.concatenate([cosines, cosines], axis=1)
    sines = jnp.concatenate([-sines, sines], axis=1)

    return pl.pallas_call(
        project,
        grid=(PAIRS,),
        out_shape=(
            jax.ShapeDtypeStruct((GROUP * HD, DW), jnp.bfloat16),
            jax.ShapeDtypeStruct((SPAN, GROUP * HD), jnp.bfloat16),
        ),
        in_specs=[
            any_space,
            pl.BlockSpec((256, DW), lambda p: (p, 0)),
            pl.BlockSpec((256, 128), lambda p: (p, 0)),
            pl.BlockSpec((SPAN, HD), lambda p: (0, 0)),
            pl.BlockSpec((SPAN, HD), lambda p: (0, 0)),
        ],
        out_specs=(any_space, pl.BlockSpec((SPAN, 256), lambda p: (0, p))),
        scratch_shapes=[pltpu.VMEM((SPAN, DW), jnp.bfloat16), dma((4,)), dma],
        compiler_params=pltpu.CompilerParams(vmem_limit_bytes=56 * 2**20),
    )(all_tokens.reshape(SPAN, DW), placed, scales, cosines, sines)


def solution(mesh):
    in_specs = (P(("rep", "tp"), None), P(), P(), P(), P(("rep", "tp"), None), P("rep"))
    out_specs = (P("tp", None), P("rep", "tp"))
    return jax.shard_map(
        per_device, mesh=mesh, in_specs=in_specs, out_specs=out_specs, check_vma=False
    )
```

time: 334 us -> 223 us (0.67)
  Pallas kernels: 0 us -> 216 us
  waiting for transfers between devices: 156 us -> 0 us
  blocking collectives: 73.1 us -> 0 us
  matrix products: 49.3 us -> 0 us
  local copies, waits for them, and re-layouts: 29.7 us -> 1.17 us
  between operations: 14.2 us -> 0.83 us
  starting transfers between devices: 4.61 us -> 0 us
    pallas_call x0 -> x2, Pallas kernels: none -> 216 us  [the longest x1 160 us: per_device(): pl.pallas_call(exchange, out_shape=(jax.ShapeDtypeStruct((16, ROWS, DW),...]
    all_gather x2 -> x0, waiting for transfers between devices: 156 us -> none  [the longest x1 94.7 us: per_device(): lax.all_gather(tokens, 'tp', axis=0, tiled=True)]
    all_to_all x1 -> x0, blocking collectives: 57.6 us -> none  [per_device(): lax.all_to_all(send_rows, 'tp', split_axis=0, concat_axis=2, tiled=True)]
    dot_general x3 -> x0, matrix products: 49.3 us -> none  [the longest x1 27.3 us: per_device(): lax.dot_general(lax.all_gather(tokens, 'tp', axis=0, tiled=True), refit_w...]
    gather x4 -> x0, local copies, waits for them, and re-layouts: 19.2 us -> none  [the longest x1 10.5 us: per_device(): jnp.take_along_axis(got_scale[0], flat_index, axis=1).reshape(-1)]
    all_gather x1 -> x0, blocking collectives: 15.5 us -> none  [per_device(): lax.all_gather(part_scale, 'rep', axis=2, tiled=True)]
    all_to_all x1 -> x0, starting transfers between devices: 4.53 us -> none  [per_device(): lax.all_to_all(send_scale, 'tp', split_axis=0, concat_axis=2, tiled=True)]
  transfers between devices with their start and end apart: 3 -> 0, of which waited for: 2 -> 0; matrix products, arithmetic and copies ran while one was open for 12% -> 0% of each run, Pallas kernels for 0% -> 0%
where the time goes in v1:
time: 223 us; the launch traced here: 222 us
  Pallas kernels  216 us (97%)
  other arithmetic  3.92 us (2%)
    pallas_call x1, Pallas kernels, per_device(): pl.pallas_call(exchange, out_shape=(jax.ShapeDtypeStruct((16, ROWS, DW),...  160 us
    pallas_call x1, Pallas kernels, per_device(): pl.pallas_call(project, grid=(PAIRS,), out_shape=(jax.ShapeDtypeStruct((G...  56.8 us

profile of v1, /device:TPU:1, one launch (start us, length us, event | category | flops | bytes accessed | tf_op | source)
XLA Modules:
  0.0 222.3 jit_solution(14213942202722076279)
XLA Ops:
  0.6 1.2 pad_bitcast_fusion.kv_row
  1.8 0.7 convert_element_type.3
  2.5 1.9 fusion
  4.4 1.3 pad_maximum_fusion
  5.7 159.6 %shard_map.77 = (bf16[16,64,8192]{2,1,0:T(8,128)(2,1)}, bf16[1280,8192]{1,0:T(8,128)(2,1)}, f32[1280,128]{1,0:T(8,128)}) custom-call(bf16[64,8192]{1,0:T(8,128)(2,1)} %tokens.1, bf16[144,8192]{1,0:T(8,128)(2,1)} %learner.1, s32[144,128]{1,0:T(8,128)} %bitcast.6, s32[1,128]{1,0:T(1,128)} %bitcast.7, s32[1,128]{1,0:T(1,128)} %pad_bitcast_fusion.kv_row, ...), custom_call_target="tpu_custom_call" | custom-call | tf_op jit(solution)/shard_map/pallas_call | solution.py:425
  165.3 56.8 %shard_map.78 = (bf16[1280,8192]{1,0:T(8,128)(2,1)}, bf16[1024,1280]{1,0:T(8,128)(2,1)}) custom-call(bf16[1024,8192]{1,0:T(8,128)(2,1)} %bitcast.5, bf16[1280,8192]{1,0:T(8,128)(2,1)} %get-tuple-element.6.weight, f32[1280,128]{1,0:T(8,128)} %get-tuple-element.7.scales, f32[1024,128]{1,0:T(8,128)} %get-tuple-element.11.cosines, ...), custom_call_target="tpu_custom_call" | custom-call | tf_op jit(solution)/shard_map/pallas_call | solution.py:471
  (1 shorter events, 0.0 us)

commit v2 on v1

--- a/solution.py
+++ b/solution.py
@@ -21,6 +21,7 @@
 QS = DW // SUB
 HALF = DW // 2
 WIDE = PAIRS * SUB + 128
+SCALES = PAIRS * SUB
 SLOTS = 2048
 
 epsilon = 1e-06
@@ -29,13 +30,11 @@
 
 
 def columns_of(pair):
-    if pair == 0:
-        return pl.ds(0, SUB + 128)
-    return pl.ds(128 + pair * SUB, SUB)
+    return pl.ds(pair * SUB, SUB + 128 if pair == PAIRS - 1 else SUB)
 
 
 def data_of(pair):
-    return pl.ds(128 + pair * SUB, SUB)
+    return pl.ds(pair * SUB, SUB)
 
 
 def exchange(
@@ -46,12 +45,17 @@
     kv_row,
     query_s,
     kv_s,
+    position_rows,
+    frequency,
     all_tokens,
     placed,
     scales,
+    cosines,
+    sines,
     rows,
     stacked,
     sending,
+    arrived,
     slab,
     stage,
     turned,
@@ -189,9 +193,7 @@
             to = place_of(dx, dz)
             pltpu.make_async_remote_copy(
                 src_ref=sending.at[pl.ds(pl.multiple_of(to * 16, 16), 16), columns_of(pair)],
-                dst_ref=slab.at[
-                    pl.ds(pl.multiple_of((core * 4 + y) * 256 + tp * 16, 16), 16), columns_of(pair)
-                ],
+                dst_ref=arrived.at[pl.ds(pl.multiple_of(tp * 16, 16), 16), columns_of(pair)],
                 send_sem=a_send.at[pair],
                 recv_sem=a_recv.at[pair],
                 device_id=(rep, to),
@@ -199,7 +201,7 @@
             ).start()
         pltpu.make_async_copy(
             sending.at[pl.ds(pl.multiple_of(tp * 16, 16), 16), columns_of(pair)],
-            slab.at[pl.ds(pl.multiple_of((core * 4 + y) * 256 + tp * 16, 16), 16), columns_of(pair)],
+            arrived.at[pl.ds(pl.multiple_of(tp * 16, 16), 16), columns_of(pair)],
             s_sem.at[pair],
         ).start()
 
@@ -207,10 +209,16 @@
     up, down, across = (rep_of(1), tp), (rep_of(-1), tp), (twin, tp)
 
     def gathered(pair):
-        fifteen = slab.at[block_rows(core, y, 0, 240), columns_of(pair)]
+        fifteen = arrived.at[pl.ds(0, 240), columns_of(pair)]
         pltpu.make_async_copy(fifteen, fifteen, a_recv.at[pair]).wait()
-        one = slab.at[block_rows(core, y, 0, 16), columns_of(pair)]
+        one = arrived.at[pl.ds(0, 16), columns_of(pair)]
         pltpu.make_async_copy(one, one, s_sem.at[pair]).wait()
+        row = lax.broadcasted_iota(jnp.int32, (256, 256), 0)
+        lane = lax.broadcasted_iota(jnp.int32, (256, 256), 1)
+        swap = jnp.where(lane == (row % 16) * 16 + row // 16, 1.0, 0.0).astype(jnp.bfloat16)
+        slab[mine, columns_of(pair)] = jnp.dot(
+            swap, arrived[:, columns_of(pair)], preferred_element_type=jnp.float32
+        ).astype(jnp.bfloat16)
         weight_copy(pair, 0, mine, w_recv.at[pair * 4], up)
         weight_copy(pair, 1, mine, w_recv.at[pair * 4 + 1], down)
         weight_copy(pair, 4, mine, c_recv.at[pair], across)
@@ -236,27 +244,40 @@
         if pair >= 2:
             stored(pair - 2).wait()
 
+        lane = lax.broadcasted_iota(jnp.int32, (HD, HD), 1)
+        none = jnp.zeros((HD, HD), jnp.float32)
+        first = jnp.where(lane == turned[:, 2 * pair : 2 * pair + 1], 1.0, 0.0)
+        second = jnp.where(lane == turned[:, 2 * pair + 1 : 2 * pair + 2], 1.0, 0.0)
+        picker = jnp.concatenate(
+            [jnp.concatenate([first, none], axis=1), jnp.concatenate([none, second], axis=1)], axis=0
+        ).astype(jnp.bfloat16)
+
+        def piece_rows(q, columns_):
+            parts = [
+                slab[pl.ds(pl.multiple_of(b * 256 + (2 * q + i) * 16, 16), 16), columns_]
+                for i in (0, 1)
+                for b in range(8)
+            ]
+            return jnp.dot(picker, jnp.concatenate(parts, axis=0), preferred_element_type=jnp.float32)
+
         def columns(q, carry):
-            lane = lax.broadcasted_iota(jnp.int32, (HD, SLOTS), 1)
-            parts = []
-            for i in (0, 1):
-                want = turned[:, pl.ds(2 * pair + i, 1)] + (2 * q + i)
-                parts.append(jnp.where(lane == want, 1.0, 0.0).astype(jnp.bfloat16))
-            picker = jnp.concatenate(parts, axis=0)
-            stage[buffer, :, pl.ds(pl.multiple_of(q * SUB, SUB), SUB)] = jnp.dot(
-                picker, slab[:, data_of(pair)], preferred_element_type=jnp.float32
+            stage[buffer, :, pl.ds(pl.multiple_of(q * SUB, SUB), SUB)] = piece_rows(
+                q, data_of(pair)
             ).astype(jnp.bfloat16)
-
-            @pl.when(q == 0)
-            def _():
-                scales[pl.ds(pair * 256, 256), :] = jnp.dot(
-                    picker, slab[:, pl.ds(0, 128)], preferred_element_type=jnp.float32
-                )
-
             return carry
 
         lax.fori_loop(0, QS, columns, 0)
         stored(pair).start()
+        return picker
+
+    def place_scales(pickers):
+        for pair in range(PAIRS):
+            parts = [
+                slab[pl.ds(b * 256 + i * 16, 16), pl.ds(SCALES, 128)] for i in (0, 1) for b in range(8)
+            ]
+            scales[pl.ds(pair * 256, 256), :] = jnp.dot(
+                pickers[pair], jnp.concatenate(parts, axis=0), preferred_element_type=jnp.float32
+            )
 
     def stored(pair):
         return pltpu.make_async_copy(
@@ -285,19 +306,12 @@
         if pair < 4:
             chosen = jnp.where(lane == u * 8 + 2 * pair + i, query_row[0:1, :], 0)
             return jnp.sum(chosen.astype(jnp.float32), axis=1, keepdims=True).astype(jnp.int32)
-        chosen = jnp.where(lane == u, kv_row[0:1, :] + QH + KVH * i, 0)
+        row = lax.broadcasted_iota(jnp.int32, (256, 16), 0)
+        lane = lax.broadcasted_iota(jnp.int32, (256, 16), 1)
+        chosen = jnp.where(lane == row // 16, kv_row[0:1, :] + QH + KVH * (row % 2), 0)
         return jnp.sum(chosen.astype(jnp.float32), axis=1, keepdims=True).astype(jnp.int32)
 
     heads = [head_column(pair) for pair in range(PAIRS)]
-    tile = jnp.zeros((256, 128), jnp.float32)
-    lane = lax.broadcasted_iota(jnp.int32, (256, HEADS), 1)
-    lane128 = lax.broadcasted_iota(jnp.int32, (256, 128), 1)
-    for pair in range(PAIRS):
-        pick = jnp.where(lane == heads[pair], 1.0, 0.0).astype(jnp.bfloat16)
-        got = jnp.dot(pick, wide_scale, preferred_element_type=jnp.float32)
-        tile = jnp.where(lane128 == pair, got, tile)
-    sending[:, pl.ds(0, 128)] = tile.astype(jnp.bfloat16)
-
     def prepare(pair):
         piece_of = (lax.broadcasted_iota(jnp.int32, (256, 1), 0) // 2) % QS
         want = heads[pair] + piece_of * HEADS
@@ -307,11 +321,22 @@
             pick, stacked[...], preferred_element_type=jnp.float32
         ).astype(jnp.bfloat16)
 
-    for pair in range(PAIRS):
+    for pair in range(PAIRS - 1):
         prepare(pair)
         scatter(pair)
         if pair == 1:
             token_step(0)
+    tile = jnp.zeros((256, 128), jnp.float32)
+    lane = lax.broadcasted_iota(jnp.int32, (256, HEADS), 1)
+    lane128 = lax.broadcasted_iota(jnp.int32, (256, 128), 1)
+    for pair in range(PAIRS):
+        pick = jnp.where(lane == heads[pair], 1.0, 0.0).astype(jnp.bfloat16)
+        got = jnp.dot(pick, wide_scale, preferred_element_type=jnp.float32)
+        tile = jnp.where(lane128 == pair, got, tile)
+    sending[:, pl.ds(SCALES, 128)] = tile.astype(jnp.bfloat16)
+
+    prepare(PAIRS - 1)
+    scatter(PAIRS - 1)
 
     turned[...] = jnp.zeros_like(turned)
     for i in range(GROUP):
@@ -321,10 +346,22 @@
             head = kv_s[tp] + QH + KVH * (i - 8)
         slot = slots[pl.ds(head, 1), :]
         source = ((slot.astype(jnp.float32) + 0.5) * (1.0 / HEADS)).astype(jnp.int32)
-        at = ((source // 16) % 2 * 4 + source // 32) * 256 + (source % 16) * 16
+        at = ((source // 16) % 2 * 4 + source // 32) * 16 + source % 16
         turned[i : i + 1, :] = at
     turned[...] = jnp.transpose(turned[...].astype(jnp.float32)).astype(jnp.int32)
 
+    def angles():
+        lines = jnp.concatenate(
+            [position_rows[...].astype(jnp.float32), jnp.zeros((HD - 8, HD), jnp.float32)], axis=0
+        )
+        lines = jnp.transpose(lines)
+        sign = jnp.where(lax.broadcasted_iota(jnp.int32, (HD, HD), 1) < HD // 2, -1.0, 1.0)
+        for k in range(8):
+            angle = lines[:, k : k + 1] * frequency[0:1, :]
+            cosines[pl.ds(k * HD, HD), :] = jnp.cos(angle)
+            sines[pl.ds(k * HD, HD), :] = jnp.sin(angle) * sign
+
+    pickers = []
     gathered(0)
     token_step(1)
     gathered(1)
@@ -332,33 +369,35 @@
     relayed(0)
     gathered(2)
     token_step(3)
+    angles()
     opposite(0)
     relayed(1)
     gathered(3)
-    crossed(0)
-    place(0)
     token_step(4)
     opposite(1)
     relayed(2)
     gathered(4)
-    crossed(1)
-    place(1)
+    crossed(0)
+    pickers.append(place(0))
     token_step(5)
     opposite(2)
     relayed(3)
-    crossed(2)
-    place(2)
+    crossed(1)
+    pickers.append(place(1))
     token_step(6)
     token_step(8)
     opposite(3)
     relayed(4)
-    crossed(3)
-    place(3)
+    crossed(2)
+    pickers.append(place(2))
     token_step(7)
     token_step(9)
+    crossed(3)
+    pickers.append(place(3))
     opposite(4)
     crossed(4)
-    place(4)
+    pickers.append(place(4))
+    place_scales(pickers)
     token_step(10)
     token_step(11)
 
@@ -397,23 +436,21 @@
         preferred_element_type=jnp.float32,
     )[0:1, :]
 
-    for k in range(4):
-
-        @pl.when(pair == 0)
-        def _():
+    @pl.when(pair == 0)
+    def _():
+        for k in range(4):
             load(k).wait()
 
-        rows = pl.ds(k * 256, 256)
-        product = lax.dot_general(
-            held[rows, :], weight[...], (((1,), (1,)), ((), ())), preferred_element_type=jnp.float32
-        )
-        product = product * column_scale
-        for i in (0, 1):
-            part = product[:, i * HD : (i + 1) * HD]
-            turn = part * cosines[rows, :] + pltpu.roll(part, HD // 2, 1) * sines[rows, :]
-            if i == 1:
-                turn = jnp.where(pair == PAIRS - 1, part, turn)
-            out[rows, pl.ds(i * HD, HD)] = turn.astype(jnp.bfloat16)
+    product = lax.dot_general(
+        held[...], weight[...], (((1,), (1,)), ((), ())), preferred_element_type=jnp.float32
+    )
+    product = product * column_scale
+    for i in (0, 1):
+        part = product[:, i * HD : (i + 1) * HD]
+        turn = part * cosines[...] + pltpu.roll(part, HD // 2, 1) * sines[...]
+        if i == 1:
+            turn = jnp.where(pair == PAIRS - 1, part, turn)
+        out[:, pl.ds(i * HD, HD)] = turn.astype(jnp.bfloat16)
     keep.wait()
 
 
@@ -422,18 +459,22 @@
     vmem = pl.BlockSpec(memory_space=pltpu.VMEM)
     smem = pl.BlockSpec(memory_space=pltpu.SMEM)
     dma = pltpu.SemaphoreType.DMA
-    all_tokens, placed, scales = pl.pallas_call(
+    frequency = jnp.exp(jnp.arange(HD // 2, dtype=jnp.float32) * (-2.0 * math.log(rope_base) / HD))
+    all_tokens, placed, scales, cosines, sines = pl.pallas_call(
         exchange,
         out_shape=(
             jax.ShapeDtypeStruct((16, ROWS, DW), jnp.bfloat16),
             jax.ShapeDtypeStruct((GROUP * HD, DW), jnp.bfloat16),
             jax.ShapeDtypeStruct((GROUP * HD, 128), jnp.float32),
+            jax.ShapeDtypeStruct((SPAN, HD), jnp.float32),
+            jax.ShapeDtypeStruct((SPAN, HD), jnp.float32),
         ),
-        in_specs=[any_space, any_space, vmem, vmem, vmem, smem, smem],
-        out_specs=(any_space, any_space, vmem),
+        in_specs=[any_space, any_space, vmem, vmem, vmem, smem, smem, vmem, vmem],
+        out_specs=(any_space, any_space, vmem, vmem, vmem),
         scratch_shapes=[
             pltpu.VMEM((HEADS, DW), jnp.bfloat16),
             pltpu.VMEM((QS * HEADS, SUB), jnp.bfloat16),
+            pltpu.VMEM((256, WIDE), jnp.bfloat16),
             pltpu.VMEM((256, WIDE), jnp.bfloat16),
             pltpu.VMEM((SLOTS, WIDE), jnp.bfloat16),
             pltpu.VMEM((2, 256, DW), jnp.bfloat16),
@@ -456,17 +497,12 @@
         learner_rows,
         learner_slot.reshape(HEADS, HD),
         query_order.reshape(1, QH),
-        jnp.pad(kv_order, (0, 128 - kv_order.shape[0])).reshape(1, 128),
+        kv_order.reshape(1, 16),
         query_order,
         kv_order,
+        positions.reshape(8, HD),
+        jnp.concatenate([frequency, frequency]).reshape(1, HD),
     )
-
-    half = HD // 2
-    frequency = jnp.exp(jnp.arange(half, dtype=jnp.float32) * (-2.0 * math.log(rope_base) / HD))
-    angles = positions.astype(jnp.float32)[:, None] * frequency[None, :]
-    cosines, sines = jnp.cos(angles), jnp.sin(angles)
-    cosines = jnp.concatenate([cosines, cosines], axis=1)
-    sines = jnp.concatenate([-sines, sines], axis=1)
 
     return pl.pallas_call(
         project,

time: 223 us -> 187 us (0.84)
  Pallas kernels: 216 us -> 186 us
  other arithmetic: 3.92 us -> 0.6 us
    pallas_call x1, Pallas kernels: 56.8 us -> 35 us  [per_device(): pl.pallas_call(project, grid=(PAIRS,), out_shape=(jax.ShapeDtypeStruct((G...]
    pallas_call x1, Pallas kernels: 160 us -> 151 us  [per_device(): pl.pallas_call(exchange, out_shape=(jax.ShapeDtypeStruct((16, ROWS, DW),...]
where the time goes in v2:
time: 187 us
  Pallas kernels  186 us (99%)
    pallas_call x1, Pallas kernels, per_device(): pl.pallas_call(exchange, out_shape=(jax.ShapeDtypeStruct((16, ROWS, DW),...  151 us
    pallas_call x1, Pallas kernels, per_device(): pl.pallas_call(project, grid=(PAIRS,), out_shape=(jax.ShapeDtypeStruct((G...  35 us

profile of v2, /device:TPU:1, one launch (start us, length us, event | category | flops | bytes accessed | tf_op | source)
XLA Modules:
  0.0 186.9 jit_solution(10521536192505248196)
XLA Ops:
  0.6 0.6 maximum_bitcast_fusion.frequency
  1.2 150.7 %shard_map.77 = (bf16[16,64,8192]{2,1,0:T(8,128)(2,1)}, bf16[1280,8192]{1,0:T(8,128)(2,1)}, f32[1280,128]{1,0:T(8,128)}, f32[1024,128]{1,0:T(8,128)}, f32[1024,128]{1,0:T(8,128)}) custom-call(bf16[64,8192]{1,0:T(8,128)(2,1)} %tokens.1, bf16[144,8192]{1,0:T(8,128)(2,1)} %learner.1, s32[144,128]{1,0:T(8,128)} %bitcast.8, s32[1,128]{1,0:T(1,128)} %bitcast.10, ...), custom_call_target="tpu_custom_call" | custom-call | tf_op jit(solution)/shard_map/pallas_call | solution.py:463
  151.9 35.0 %shard_map.78 = (bf16[1280,8192]{1,0:T(8,128)(2,1)}, bf16[1024,1280]{1,0:T(8,128)(2,1)}) custom-call(bf16[1024,8192]{1,0:T(8,128)(2,1)} %bitcast.7, bf16[1280,8192]{1,0:T(8,128)(2,1)} %get-tuple-element.8.weight, f32[1280,128]{1,0:T(8,128)} %get-tuple-element.9.scales, f32[1024,128]{1,0:T(8,128)} %get-tuple-element.10.cosines, ...), custom_call_target="tpu_custom_call" | custom-call | tf_op jit(solution)/shard_map/pallas_call | solution.py:507
  (1 shorter events, 0.0 us)

commit v3 on v2

--- a/solution.py
+++ b/solution.py
@@ -21,7 +21,7 @@
 QS = DW // SUB
 HALF = DW // 2
 WIDE = PAIRS * SUB + 128
-SCALES = PAIRS * SUB
+SCALES = 2 * SUB
 SLOTS = 2048
 
 epsilon = 1e-06
@@ -30,11 +30,30 @@
 
 
 def columns_of(pair):
-    return pl.ds(pair * SUB, SUB + 128 if pair == PAIRS - 1 else SUB)
+    return pl.ds(pair * SUB + (128 if pair > 1 else 0), SUB + 128 if pair == 1 else SUB)
 
 
 def data_of(pair):
-    return pl.ds(pair * SUB, SUB)
+    return pl.ds(pair * SUB + (128 if pair > 1 else 0), SUB)
+
+
+def place_at(x, z, dx, dz):
+    return lax.rem(x + dx + 4, 4) * 4 + lax.rem(z + dz + 4, 4)
+
+
+EARLY = ((0, 0), (1, 0), (-1, 0), (0, 1), (0, -1), (-1, -1), (1, 1), (1, -1), (-1, 1))
+LATE = ((2, 0), (0, 2), (2, -1), (2, 1), (-1, 2), (1, 2), (2, 2))
+E_ROWS = len(EARLY) * ROWS
+L_ROWS = len(LATE) * ROWS
+
+
+def rotated(product, scale, cosines, sines, is_value):
+    parts = []
+    for i in (0, 1):
+        part = product[:, i * HD : (i + 1) * HD] * scale[:, i * HD : (i + 1) * HD]
+        turn = part * cosines + pltpu.roll(part, HD // 2, 1) * sines
+        parts.append(turn if i == 0 else jnp.where(is_value, part, turn))
+    return parts
 
 
 def exchange(
@@ -49,9 +68,10 @@
     frequency,
     all_tokens,
     placed,
-    scales,
-    cosines,
-    sines,
+    scale_rows,
+    early,
+    cosines_late,
+    sines_late,
     rows,
     stacked,
     sending,
@@ -59,6 +79,13 @@
     slab,
     stage,
     turned,
+    pickers,
+    cosines,
+    sines,
+    cosines_early,
+    sines_early,
+    held,
+    result,
     t_send,
     t_recv,
     w_send,
@@ -68,6 +95,8 @@
     c_recv,
     l_sem,
     s_sem,
+    e_sem,
+    o_sem,
 ):
     rep = lax.axis_index("rep")
     tp = lax.axis_index("tp")
@@ -75,7 +104,7 @@
     x, z = tp // 4, tp % 4
 
     def place_of(dx, dz):
-        return lax.rem(x + dx + 4, 4) * 4 + lax.rem(z + dz + 4, 4)
+        return place_at(x, z, dx, dz)
 
     def rep_of(dy):
         return lax.rem(y + dy + 4, 4) * 2 + core
@@ -107,7 +136,7 @@
     started = []
 
     def token_copy(half, number, block, low, count, phase, step, own=False):
-        k = half * 20 + number
+        k = half * 22 + number
         source = piece(tokens, half, low, count) if own else piece(all_tokens.at[block], half, low, count)
         copy = pltpu.make_async_remote_copy(
             src_ref=source,
@@ -121,14 +150,15 @@
         started.append(copy)
 
     def token_wait(half, number, block, low, count):
-        k = half * 20 + number
+        k = half * 22 + number
         here = piece(all_tokens.at[block], half, low, count)
         pltpu.make_async_copy(here, here, t_recv.at[k]).wait()
 
-    def first_sends():
+    def first_sends(part):
+        low = part * ROWS // 2
         for half in (0, 1):
-            token_copy(half, 0, tp, 0, ROWS, 0, 1, own=True)
-            token_copy(half, 1, tp, 0, ROWS, 0, -1, own=True)
+            token_copy(half, 20 * part, tp, low, ROWS // 2, 0, 1, own=True)
+            token_copy(half, 20 * part + 1, tp, low, ROWS // 2, 0, -1, own=True)
 
     order = (0, -1, 1, 2)
 
@@ -143,12 +173,14 @@
                 second_sends(half, 0)
             elif number == 1:
                 block = block_at(half, -1, 0)
-                token_wait(half, 0, block, 0, ROWS)
+                token_wait(half, 0, block, 0, ROWS // 2)
+                token_wait(half, 20, block, ROWS // 2, ROWS // 2)
                 token_copy(half, 2, block, 0, ROWS // 2, 0, 1)
                 second_sends(half, 1)
             elif number == 2:
                 block = block_at(half, 1, 0)
-                token_wait(half, 1, block, 0, ROWS)
+                token_wait(half, 1, block, 0, ROWS // 2)
+                token_wait(half, 21, block, ROWS // 2, ROWS // 2)
                 token_copy(half, 3, block, ROWS // 2, ROWS // 2, 0, -1)
                 second_sends(half, 2)
             elif number == 3:
@@ -244,21 +276,13 @@
         if pair >= 2:
             stored(pair - 2).wait()
 
-        lane = lax.broadcasted_iota(jnp.int32, (HD, HD), 1)
-        none = jnp.zeros((HD, HD), jnp.float32)
-        first = jnp.where(lane == turned[:, 2 * pair : 2 * pair + 1], 1.0, 0.0)
-        second = jnp.where(lane == turned[:, 2 * pair + 1 : 2 * pair + 2], 1.0, 0.0)
-        picker = jnp.concatenate(
-            [jnp.concatenate([first, none], axis=1), jnp.concatenate([none, second], axis=1)], axis=0
-        ).astype(jnp.bfloat16)
-
         def piece_rows(q, columns_):
             parts = [
                 slab[pl.ds(pl.multiple_of(b * 256 + (2 * q + i) * 16, 16), 16), columns_]
                 for i in (0, 1)
                 for b in range(8)
             ]
-            return jnp.dot(picker, jnp.concatenate(parts, axis=0), preferred_element_type=jnp.float32)
+            return jnp.dot(pickers[pair], jnp.concatenate(parts, axis=0), preferred_element_type=jnp.float32)
 
         def columns(q, carry):
             stage[buffer, :, pl.ds(pl.multiple_of(q * SUB, SUB), SUB)] = piece_rows(
@@ -268,23 +292,72 @@
 
         lax.fori_loop(0, QS, columns, 0)
         stored(pair).start()
-        return picker
-
-    def place_scales(pickers):
+
+    def make_pickers():
+        lane = lax.broadcasted_iota(jnp.int32, (HD, HD), 1)
+        none = jnp.zeros((HD, HD), jnp.float32)
         for pair in range(PAIRS):
-            parts = [
-                slab[pl.ds(b * 256 + i * 16, 16), pl.ds(SCALES, 128)] for i in (0, 1) for b in range(8)
-            ]
-            scales[pl.ds(pair * 256, 256), :] = jnp.dot(
-                pickers[pair], jnp.concatenate(parts, axis=0), preferred_element_type=jnp.float32
+            first = jnp.where(lane == turned[:, 2 * pair : 2 * pair + 1], 1.0, 0.0)
+            second = jnp.where(lane == turned[:, 2 * pair + 1 : 2 * pair + 2], 1.0, 0.0)
+            pickers[pair] = jnp.concatenate(
+                [jnp.concatenate([first, none], axis=1), jnp.concatenate([none, second], axis=1)], axis=0
+            ).astype(jnp.bfloat16)
+
+    def place_scales():
+        lane = lax.broadcasted_iota(jnp.int32, (8, 128), 1)
+        parts = [slab[pl.ds(b * 256 + i * 16, 16), pl.ds(SCALES, 128)] for i in (0, 1) for b in range(8)]
+        tiles = jnp.concatenate(parts, axis=0)
+        for pair in range(PAIRS):
+            column = jnp.dot(pickers[pair], tiles, preferred_element_type=jnp.float32)
+            chosen = jnp.where(lane == pair, 1.0, 0.0).astype(jnp.bfloat16)
+            scale_rows[pl.ds(pair * 8, 8), :] = lax.dot_general(
+                chosen,
+                column.astype(jnp.bfloat16),
+                (((1,), (1,)), ((), ())),
+                preferred_element_type=jnp.float32,
             )
+
+    def early_load(k):
+        block = place_of(*EARLY[k])
+        return pltpu.make_async_copy(all_tokens.at[block], held.at[pl.ds(k * ROWS, ROWS)], e_sem.at[k])
+
+    def load_early(low, high):
+        if low == 0:
+            own_copy.wait()
+        for k in range(low, high):
+            early_load(k).start()
+
+    def early_out(pair):
+        return pltpu.make_async_copy(
+            result.at[pair % 2], early.at[:, pl.ds(pair * 256, 256)], o_sem.at[pair % 2]
+        )
+
+    def multiply(pair):
+        if pair == 0:
+            for k in range(len(EARLY)):
+                early_load(k).wait()
+        if pair >= 2:
+            early_out(pair - 2).wait()
+        product = lax.dot_general(
+            held[...], stage[pair % 2], (((1,), (1,)), ((), ())), preferred_element_type=jnp.float32
+        )
+        parts = rotated(
+            product,
+            scale_rows[pl.ds(pair * 8, 1), :],
+            cosines_early[...],
+            sines_early[...],
+            pair == PAIRS - 1,
+        )
+        for i in (0, 1):
+            result[pair % 2, :, pl.ds(i * HD, HD)] = parts[i].astype(jnp.bfloat16)
+        early_out(pair).start()
 
     def stored(pair):
         return pltpu.make_async_copy(
             stage.at[pair % 2], placed.at[pl.ds(pair * 256, 256)], l_sem.at[2 + pair % 2]
         )
 
-    first_sends()
+    first_sends(0)
     load_rows.wait()
 
     largest = jnp.zeros((HEADS, 1), jnp.float32)
@@ -321,11 +394,9 @@
             pick, stacked[...], preferred_element_type=jnp.float32
         ).astype(jnp.bfloat16)
 
-    for pair in range(PAIRS - 1):
-        prepare(pair)
-        scatter(pair)
-        if pair == 1:
-            token_step(0)
+    prepare(0)
+    scatter(0)
+    first_sends(1)
     tile = jnp.zeros((256, 128), jnp.float32)
     lane = lax.broadcasted_iota(jnp.int32, (256, HEADS), 1)
     lane128 = lax.broadcasted_iota(jnp.int32, (256, 128), 1)
@@ -335,8 +406,15 @@
         tile = jnp.where(lane128 == pair, got, tile)
     sending[:, pl.ds(SCALES, 128)] = tile.astype(jnp.bfloat16)
 
-    prepare(PAIRS - 1)
-    scatter(PAIRS - 1)
+    prepare(1)
+    scatter(1)
+    prepare(2)
+    scatter(2)
+    prepare(3)
+    scatter(3)
+    prepare(4)
+    scatter(4)
+    token_step(0)
 
     turned[...] = jnp.zeros_like(turned)
     for i in range(GROUP):
@@ -360,50 +438,65 @@
             angle = lines[:, k : k + 1] * frequency[0:1, :]
             cosines[pl.ds(k * HD, HD), :] = jnp.cos(angle)
             sines[pl.ds(k * HD, HD), :] = jnp.sin(angle) * sign
-
-    pickers = []
+        for blocks, c_ref, s_ref in (
+            (EARLY, cosines_early, sines_early),
+            (LATE, cosines_late, sines_late),
+        ):
+            for k, offset in enumerate(blocks):
+                there = pl.ds(pl.multiple_of(place_of(*offset) * ROWS, ROWS), ROWS)
+                c_ref[pl.ds(k * ROWS, ROWS), :] = cosines[there, :]
+                s_ref[pl.ds(k * ROWS, ROWS), :] = sines[there, :]
+
+    make_pickers()
+    token_step(1)
+    token_step(2)
     gathered(0)
-    token_step(1)
     gathered(1)
-    token_step(2)
+    gathered(2)
     relayed(0)
-    gathered(2)
+    gathered(3)
+    angles()
+    relayed(1)
+    gathered(4)
+    relayed(2)
+    token_step(4)
+    opposite(0)
+    crossed(0)
+    place(0)
+    relayed(3)
     token_step(3)
-    angles()
-    opposite(0)
-    relayed(1)
-    gathered(3)
-    token_step(4)
+    token_step(5)
     opposite(1)
-    relayed(2)
-    gathered(4)
-    crossed(0)
-    pickers.append(place(0))
-    token_step(5)
+    crossed(1)
+    place(1)
+    place_scales()
+    token_step(6)
+    load_early(0,9)
+    relayed(4)
+    multiply(0)
+    multiply(1)
+    token_step(8)
     opposite(2)
-    relayed(3)
-    crossed(1)
-    pickers.append(place(1))
-    token_step(6)
-    token_step(8)
+    crossed(2)
+    place(2)
+    token_step(7)
+    multiply(2)
     opposite(3)
-    relayed(4)
-    crossed(2)
-    pickers.append(place(2))
-    token_step(7)
-    token_step(9)
     crossed(3)
-    pickers.append(place(3))
+    place(3)
+    multiply(3)
     opposite(4)
     crossed(4)
-    pickers.append(place(4))
-    place_scales(pickers)
+    place(4)
+    multiply(4)
+    token_step(9)
     token_step(10)
     token_step(11)
 
-    own_copy.wait()
     stored(3).wait()
     stored(4).wait()
+    early_out(3).wait()
+    early_out(4).wait()
     for copy in started:
         copy.wait_send()
     for pair in range(PAIRS):
@@ -411,46 +504,43 @@
         pltpu.make_async_copy(fifteen, fifteen, a_send.at[pair]).wait()
 
 
-def project(tokens, weight, scales, cosines, sines, refit, out, held, t_sem, r_sem):
+def project(tokens, weight, scale_rows, early, cosines, sines, refit, out, held, t_sem, r_sem):
     pair = pl.program_id(0)
+    tp = lax.axis_index("tp")
+    x, z = tp // 4, tp % 4
 
     def load(k):
         return pltpu.make_async_copy(
-            tokens.at[pl.ds(k * 256, 256)], held.at[pl.ds(k * 256, 256)], t_sem.at[k]
+            tokens.at[place_at(x, z, *LATE[k])], held.at[pl.ds(k * ROWS, ROWS)], t_sem.at[k]
         )
 
     @pl.when(pair == 0)
     def _():
-        for k in range(4):
+        for k in range(len(LATE)):
             load(k).start()
 
     keep = pltpu.make_async_copy(weight, refit.at[pl.ds(pl.multiple_of(pair * 256, 256), 256)], r_sem)
     keep.start()
 
-    lane = lax.broadcasted_iota(jnp.int32, (8, 128), 1)
-    chosen = jnp.where(lane == pair, 1.0, 0.0).astype(jnp.bfloat16)
-    column_scale = lax.dot_general(
-        chosen,
-        scales[...].astype(jnp.bfloat16),
-        (((1,), (1,)), ((), ())),
-        preferred_element_type=jnp.float32,
-    )[0:1, :]
+    def rows_at(offset):
+        return pl.ds(pl.multiple_of(place_at(x, z, *offset) * ROWS, ROWS), ROWS)
+
+    for k, offset in enumerate(EARLY):
+        out[rows_at(offset), :] = early[pl.ds(k * ROWS, ROWS), :]
 
     @pl.when(pair == 0)
     def _():
-        for k in range(4):
+        for k in range(len(LATE)):
             load(k).wait()
 
     product = lax.dot_general(
         held[...], weight[...], (((1,), (1,)), ((), ())), preferred_element_type=jnp.float32
     )
-    product = product * column_scale
+    parts = rotated(product, scale_rows[0:1, :], cosines[...], sines[...], pair == PAIRS - 1)
     for i in (0, 1):
-        part = product[:, i * HD : (i + 1) * HD]
-        turn = part * cosines[...] + pltpu.roll(part, HD // 2, 1) * sines[...]
-        if i == 1:
-            turn = jnp.where(pair == PAIRS - 1, part, turn)
-        out[:, pl.ds(i * HD, HD)] = turn.astype(jnp.bfloat16)
+        part = parts[i].astype(jnp.bfloat16)
+        for k, offset in enumerate(LATE):
+            out[rows_at(offset), pl.ds(i * HD, HD)] = part[k * ROWS : (k + 1) * ROWS]
     keep.wait()
 
 
@@ -460,17 +550,18 @@
     smem = pl.BlockSpec(memory_space=pltpu.SMEM)
     dma = pltpu.SemaphoreType.DMA
     frequency = jnp.exp(jnp.arange(HD // 2, dtype=jnp.float32) * (-2.0 * math.log(rope_base) / HD))
-    all_tokens, placed, scales, cosines, sines = pl.pallas_call(
+    all_tokens, placed, scale_rows, early, cosines, sines = pl.pallas_call(
         exchange,
         out_shape=(
             jax.ShapeDtypeStruct((16, ROWS, DW), jnp.bfloat16),
             jax.ShapeDtypeStruct((GROUP * HD, DW), jnp.bfloat16),
-            jax.ShapeDtypeStruct((GROUP * HD, 128), jnp.float32),
-            jax.ShapeDtypeStruct((SPAN, HD), jnp.float32),
-            jax.ShapeDtypeStruct((SPAN, HD), jnp.float32),
+            jax.ShapeDtypeStruct((PAIRS * 8, 256), jnp.float32),
+            jax.ShapeDtypeStruct((E_ROWS, GROUP * HD), jnp.bfloat16),
+            jax.ShapeDtypeStruct((L_ROWS, HD), jnp.float32),
+            jax.ShapeDtypeStruct((L_ROWS, HD), jnp.float32),
         ),
         in_specs=[any_space, any_space, vmem, vmem, vmem, smem, smem, vmem, vmem],
-        out_specs=(any_space, any_space, vmem, vmem, vmem),
+        out_specs=(any_space, any_space, vmem, any_space, vmem, vmem),
         scratch_shapes=[
             pltpu.VMEM((HEADS, DW), jnp.bfloat16),
             pltpu.VMEM((QS * HEADS, SUB), jnp.bfloat16),
@@ -479,8 +570,15 @@
             pltpu.VMEM((SLOTS, WIDE), jnp.bfloat16),
             pltpu.VMEM((2, 256, DW), jnp.bfloat16),
             pltpu.VMEM((HD, HD), jnp.int32),
-            dma((40,)),
-            dma((40,)),
+            pltpu.VMEM((PAIRS, 256, 256), jnp.bfloat16),
+            pltpu.VMEM((SPAN, HD), jnp.float32),
+            pltpu.VMEM((SPAN, HD), jnp.float32),
+            pltpu.VMEM((E_ROWS, HD), jnp.float32),
+            pltpu.VMEM((E_ROWS, HD), jnp.float32),
+            pltpu.VMEM((E_ROWS, DW), jnp.bfloat16),
+            pltpu.VMEM((2, E_ROWS, 256), jnp.bfloat16),
+            dma((44,)),
+            dma((44,)),
             dma((40,)),
             dma((20,)),
             dma((PAIRS,)),
@@ -488,9 +586,11 @@
             dma((PAIRS,)),
             dma((4,)),
             dma((PAIRS,)),
+            dma((len(EARLY),)),
+            dma((2,)),
         ],
         compiler_params=pltpu.CompilerParams(
-            collective_id=0, has_side_effects=True, vmem_limit_bytes=56 * 2**20
+            collective_id=0, has_side_effects=True, vmem_limit_bytes=62 * 2**20
         ),
     )(
         tokens,
@@ -514,14 +614,15 @@
         in_specs=[
             any_space,
             pl.BlockSpec((256, DW), lambda p: (p, 0)),
-            pl.BlockSpec((256, 128), lambda p: (p, 0)),
-            pl.BlockSpec((SPAN, HD), lambda p: (0, 0)),
-            pl.BlockSpec((SPAN, HD), lambda p: (0, 0)),
+            pl.BlockSpec((8, 256), lambda p: (p, 0)),
+            pl.BlockSpec((E_ROWS, 256), lambda p: (0, p)),
+            pl.BlockSpec((L_ROWS, HD), lambda p: (0, 0)),
+            pl.BlockSpec((L_ROWS, HD), lambda p: (0, 0)),
         ],
         out_specs=(any_space, pl.BlockSpec((SPAN, 256), lambda p: (0, p))),
-        scratch_shapes=[pltpu.VMEM((SPAN, DW), jnp.bfloat16), dma((4,)), dma],
-        compiler_params=pltpu.CompilerParams(vmem_limit_bytes=56 * 2**20),
-    )(all_tokens.reshape(SPAN, DW), placed, scales, cosines, sines)
+        scratch_shapes=[pltpu.VMEM((L_ROWS, DW), jnp.bfloat16), dma((len(LATE),)), dma],
+        compiler_params=pltpu.CompilerParams(vmem_limit_bytes=62 * 2**20),
+    )(all_tokens, placed, scale_rows, early, cosines, sines)
 
 
 def solution(mesh):

time: 187 us -> 159 us (0.85)
  Pallas kernels: 186 us -> 158 us
    pallas_call x1, Pallas kernels: 151 us -> 134 us  [per_device(): pl.pallas_call(exchange, out_shape=(jax.ShapeDtypeStruct((16, ROWS, DW),...]
    pallas_call x1, Pallas kernels: 35 us -> 23.4 us  [per_device(): pl.pallas_call(project, grid=(PAIRS,), out_shape=(jax.ShapeDtypeStruct((G...]
where the time goes in v3:
time: 159 us
  Pallas kernels  158 us (99%)
    pallas_call x1, Pallas kernels, per_device(): pl.pallas_call(exchange, out_shape=(jax.ShapeDtypeStruct((16, ROWS, DW),...  134 us
    pallas_call x1, Pallas kernels, per_device(): pl.pallas_call(project, grid=(PAIRS,), out_shape=(jax.ShapeDtypeStruct((G...  23.4 us

profile of v3, /device:TPU:1, one launch (start us, length us, event | category | flops | bytes accessed | tf_op | source)
XLA Modules:
  0.0 159.2 jit_solution(8859976781934549954)
XLA Ops:
  0.6 0.6 maximum_bitcast_fusion.frequency
  1.2 134.4 %shard_map.77 = (bf16[16,64,8192]{2,1,0:T(8,128)(2,1)}, bf16[1280,8192]{1,0:T(8,128)(2,1)}, f32[40,256]{1,0:T(8,128)}, bf16[576,1280]{1,0:T(8,128)(2,1)}, f32[448,128]{1,0:T(8,128)}, /*index=5*/f32[448,128]{1,0:T(8,128)}) custom-call(bf16[64,8192]{1,0:T(8,128)(2,1)} %tokens.1, bf16[144,8192]{1,0:T(8,128)(2,1)} %learner.1, s32[144,128]{1,0:T(8,128)} %bitcast.6, ...), custom_call_target="tpu_custom_call" | custom-call | tf_op jit(solution)/shard_map/pallas_call | solution.py:553
  135.6 23.4 %shard_map.78 = (bf16[1280,8192]{1,0:T(8,128)(2,1)}, bf16[1024,1280]{1,0:T(8,128)(2,1)}) custom-call(bf16[16,64,8192]{2,1,0:T(8,128)(2,1)} %get-tuple-element.8.tokens, bf16[1280,8192]{1,0:T(8,128)(2,1)} %get-tuple-element.9.weight, f32[40,256]{1,0:T(8,128)} %get-tuple-element.10.scale_rows, bf16[576,1280]{1,0:T(8,128)(2,1)} %get-tuple-element.11.early, ...), custom_call_target="tpu_custom_call" | custom-call | tf_op jit(solution)/shard_map/pallas_call | solution.py:607
  (1 shorter events, 0.0 us)

commit v4 on v3

--- a/solution.py
+++ b/solution.py
@@ -3,6 +3,7 @@
 
 import jax
 import jax.numpy as jnp
+import numpy as np
 from jax import lax
 from jax.experimental import pallas as pl
 from jax.experimental.pallas import tpu as pltpu
@@ -113,8 +114,6 @@
 
     load_rows = pltpu.make_async_copy(learner, rows, l_sem.at[0])
     load_rows.start()
-    own_copy = pltpu.make_async_copy(tokens, all_tokens.at[tp], l_sem.at[1])
-    own_copy.start()
 
     barrier = pltpu.get_barrier_semaphore()
     offsets = [(dx, dz) for dx in (1, 3, 0, 2) for dz in (1, 3, 0, 2) if (dx, dz) != (0, 0)]
@@ -318,12 +317,10 @@
             )
 
     def early_load(k):
-        block = place_of(*EARLY[k])
-        return pltpu.make_async_copy(all_tokens.at[block], held.at[pl.ds(k * ROWS, ROWS)], e_sem.at[k])
+        source = tokens if k == 0 else all_tokens.at[place_of(*EARLY[k])]
+        return pltpu.make_async_copy(source, held.at[pl.ds(k * ROWS, ROWS)], e_sem.at[k])
 
     def load_early(low, high):
-        if low == 0:
-            own_copy.wait()
         for k in range(low, high):
             early_load(k).start()
 
@@ -480,12 +477,12 @@
     crossed(2)
     place(2)
     token_step(7)
+    opposite(3)
     multiply(2)
-    opposite(3)
     crossed(3)
     place(3)
+    opposite(4)
     multiply(3)
-    opposite(4)
     crossed(4)
     place(4)
     multiply(4)
@@ -504,7 +501,9 @@
         pltpu.make_async_copy(fifteen, fifteen, a_send.at[pair]).wait()
 
 
-def project(tokens, weight, scale_rows, early, cosines, sines, refit, out, held, t_sem, r_sem):
+def project(
+    tokens, placed, scale_rows, early, cosines, sines, refit, out, held, weight, t_sem, w_sem, r_sem
+):
     pair = pl.program_id(0)
     tp = lax.axis_index("tp")
     x, z = tp // 4, tp % 4
@@ -514,13 +513,24 @@
             tokens.at[place_at(x, z, *LATE[k])], held.at[pl.ds(k * ROWS, ROWS)], t_sem.at[k]
         )
 
+    def fetch(p):
+        return pltpu.make_async_copy(placed.at[pl.ds(p * 256, 256)], weight.at[p], w_sem.at[p])
+
+    def keep(p):
+        there = refit.at[pl.ds(pl.multiple_of(p * 256, 256), 256)]
+        return pltpu.make_async_copy(weight.at[p], there, r_sem.at[p])
+
     @pl.when(pair == 0)
     def _():
+        fetch(0).start()
         for k in range(len(LATE)):
             load(k).start()
-
-    keep = pltpu.make_async_copy(weight, refit.at[pl.ds(pl.multiple_of(pair * 256, 256), 256)], r_sem)
-    keep.start()
+        for p in range(1, PAIRS):
+            fetch(p).start()
+
+    there = weight.at[pair]
+    pltpu.make_async_copy(there, there, w_sem.at[pair]).wait()
+    keep(pair).start()
 
     def rows_at(offset):
         return pl.ds(pl.multiple_of(place_at(x, z, *offset) * ROWS, ROWS), ROWS)
@@ -534,14 +544,18 @@
             load(k).wait()
 
     product = lax.dot_general(
-        held[...], weight[...], (((1,), (1,)), ((), ())), preferred_element_type=jnp.float32
+        held[...], weight[pair], (((1,), (1,)), ((), ())), preferred_element_type=jnp.float32
     )
     parts = rotated(product, scale_rows[0:1, :], cosines[...], sines[...], pair == PAIRS - 1)
     for i in (0, 1):
         part = parts[i].astype(jnp.bfloat16)
         for k, offset in enumerate(LATE):
             out[rows_at(offset), pl.ds(i * HD, HD)] = part[k * ROWS : (k + 1) * ROWS]
-    keep.wait()
+
+    @pl.when(pair == PAIRS - 1)
+    def _():
+        for p in range(PAIRS):
+            keep(p).wait()
 
 
 def per_device(learner_rows, learner_slot, query_order, kv_order, tokens, positions):
@@ -549,7 +563,8 @@
     vmem = pl.BlockSpec(memory_space=pltpu.VMEM)
     smem = pl.BlockSpec(memory_space=pltpu.SMEM)
     dma = pltpu.SemaphoreType.DMA
-    frequency = jnp.exp(jnp.arange(HD // 2, dtype=jnp.float32) * (-2.0 * math.log(rope_base) / HD))
+    steps = np.arange(HD // 2, dtype=np.float32) * np.float32(-2.0 * math.log(rope_base) / HD)
+    frequency = np.exp(steps).astype(np.float32)
     all_tokens, placed, scale_rows, early, cosines, sines = pl.pallas_call(
         exchange,
         out_shape=(
@@ -601,7 +616,7 @@
         query_order,
         kv_order,
         positions.reshape(8, HD),
-        jnp.concatenate([frequency, frequency]).reshape(1, HD),
+        jnp.asarray(np.concatenate([frequency, frequency]).reshape(1, HD)),
     )
 
     return pl.pallas_call(
@@ -613,14 +628,20 @@
         ),
         in_specs=[
             any_space,
-            pl.BlockSpec((256, DW), lambda p: (p, 0)),
+            any_space,
             pl.BlockSpec((8, 256), lambda p: (p, 0)),
             pl.BlockSpec((E_ROWS, 256), lambda p: (0, p)),
             pl.BlockSpec((L_ROWS, HD), lambda p: (0, 0)),
             pl.BlockSpec((L_ROWS, HD), lambda p: (0, 0)),
         ],
         out_specs=(any_space, pl.BlockSpec((SPAN, 256), lambda p: (0, p))),
-        scratch_shapes=[pltpu.VMEM((L_ROWS, DW), jnp.bfloat16), dma((len(LATE),)), dma],
+        scratch_shapes=[
+            pltpu.VMEM((L_ROWS, DW), jnp.bfloat16),
+            pltpu.VMEM((PAIRS, 256, DW), jnp.bfloat16),
+            dma((len(LATE),)),
+            dma((PAIRS,)),
+            dma((PAIRS,)),
+        ],
         compiler_params=pltpu.CompilerParams(vmem_limit_bytes=62 * 2**20),
     )(all_tokens, placed, scale_rows, early, cosines, sines)
 

time: 159 us -> 155 us (0.975)
  Pallas kernels: 158 us -> 154 us
    pallas_call x1, Pallas kernels: 134 us -> 131 us  [per_device(): pl.pallas_call(exchange, out_shape=(jax.ShapeDtypeStruct((16, ROWS, DW),...]
where the time goes in v4:
time: 155 us
  Pallas kernels  154 us (99%)
    pallas_call x1, Pallas kernels, per_device(): pl.pallas_call(exchange, out_shape=(jax.ShapeDtypeStruct((16, ROWS, DW),...  131 us
    pallas_call x1, Pallas kernels, per_device(): pl.pallas_call(project, grid=(PAIRS,), out_shape=(jax.ShapeDtypeStruct((G...  22.9 us

profile of v4, /device:TPU:1, one launch (start us, length us, event | category | flops | bytes accessed | tf_op | source)
XLA Modules:
  0.0 154.8 jit_solution(5524116099795974113)
XLA Ops:
  0.6 131.1 %shard_map.86 = (bf16[16,64,8192]{2,1,0:T(8,128)(2,1)}, bf16[1280,8192]{1,0:T(8,128)(2,1)}, f32[40,256]{1,0:T(8,128)}, bf16[576,1280]{1,0:T(8,128)(2,1)}, f32[448,128]{1,0:T(8,128)}, /*index=5*/f32[448,128]{1,0:T(8,128)}) custom-call(bf16[64,8192]{1,0:T(8,128)(2,1)} %tokens.1, bf16[144,8192]{1,0:T(8,128)(2,1)} %learner.1, s32[144,128]{1,0:T(8,128)} %bitcast.4, ...), custom_call_target="tpu_custom_call" | custom-call | tf_op jit(solution)/shard_map/pallas_call | solution.py:568
  131.8 22.9 %shard_map.87 = (bf16[1280,8192]{1,0:T(8,128)(2,1)}, bf16[1024,1280]{1,0:T(8,128)(2,1)}) custom-call(bf16[16,64,8192]{2,1,0:T(8,128)(2,1)} %get-tuple-element.8.tokens, bf16[1280,8192]{1,0:T(8,128)(2,1)} %get-tuple-element.9.placed, f32[40,256]{1,0:T(8,128)} %get-tuple-element.10.scale_rows, bf16[576,1280]{1,0:T(8,128)(2,1)} %get-tuple-element.11.early, ...), custom_call_target="tpu_custom_call" | custom-call | tf_op jit(solution)/shard_map/pallas_call | solution.py:622
